TPU v7x, 256 devices: a whole 4x4x8 slice. The times are simulated.
256 devices in a mesh: sample: 16 (over x_lo, z), feat: 16 (over x_hi, y, core).
Axes of the slice: x: 4 (x_hi: 2, x_lo: 2; x = x_hi * 2 + x_lo), y: 4, z: 8, core: 2. Of those that a mesh axis runs over, the one named last changes fastest.
Arguments:
- features: bfloat16 [16384, 8192], P('sample', 'feat'), may hold values from -6 to 6
- panel: bfloat16 [8192, 1024], P('feat'), may hold values from -0.0625 to 0.0625
Outputs:
- update: float32 [8192, 1024], P('feat')
All inputs are finite; a program needn't handle non-finite values.
Results may differ from a plain program's by a relative error of at most 0.0028.
Values may be sent and summed in bfloat16 or wider, within the bound.
A program may use at most 64 MiB of HBM per device.

v0:
```python
import math

import jax
import jax.numpy as jnp
from jax import lax
from jax.sharding import PartitionSpec as P

D = 8192


def penalize(panel_rows, upper_high, upper_low):
    return jnp.dot(panel_rows, upper_high, preferred_element_type=jnp.float32) + jnp.dot(
        panel_rows, upper_low, preferred_element_type=jnp.float32
    )


def body(features, panel):
    rows, width = features.shape
    n_sample = lax.axis_size("sample")
    total = rows * n_sample
    scale_factor = math.sqrt(D)
    share = lax.psum_scatter(
        jnp.dot(features, panel, preferred_element_type=jnp.float32),
        "feat",
        scatter_dimension=0,
        tiled=True,
    ).astype(jnp.bfloat16)
    projected = lax.all_gather(share, "feat", axis=0, tiled=True)
    partial_gram = jnp.dot(projected.T, projected, preferred_element_type=jnp.float32)
    gram = lax.psum(partial_gram, "sample") / total
    upper = jnp.triu(gram)
    upper_high = lax.optimization_barrier(upper.astype(jnp.bfloat16))
    upper_low = (upper - upper_high.astype(jnp.float32)).astype(jnp.bfloat16)
    local_cross = lax.dot_general(
        features, projected, (((0,), (0,)), ((), ())), preferred_element_type=jnp.float32
    )
    cross = lax.psum(local_cross, "sample") / total
    penalty = penalize(panel, upper_high, upper_low)
    return (cross - penalty) * scale_factor


def solution(mesh):
    return jax.shard_map(
        body,
        mesh=mesh,
        in_specs=(P("sample", "feat"), P("feat", None)),
        out_specs=P("feat", None),
        check_vma=False,
    )
```

profile of v0, /device:TPU:2, one launch (start us, length us, event | category | flops | bytes accessed | tf_op | source)
XLA Modules:
  0.0 347.2 jit_solution(9680926919712552049)
XLA Ops:
  6.5 0.0 copy-start
  6.5 0.0 reduce-scatter.2.cloned.1.call-start
  6.5 1.2 copy-done
  7.8 4.4 %fusion.8 = f32[1024,1024]{1,0:T(8,128)} fusion(bf16[1024,512]{1,0:T(8,128)(2,1)} %param.2, bf16[512,1024]{1,0:T(8,128)(2,1)S(1)} %copy-done), kind=kOutput, calls=%fused_computation.14 | convolution fusion | flops 1073741824 | bytes 6291456 | tf_op jit(solution)/shard_map/dot_general | solution.py:23
  12.2 0.0 reduce-scatter.2.cloned.1.call-update
  12.2 0.0 all-gather.2.cloned.1.call-start
  12.3 90.3 %reduce-scatter.2.cloned.1.call-done = f32[64,1024]{1,0:T(8,128)} async-done(((f32[1024,1024]{1,0:T(8,128)}), f32[64,1024]{1,0:T(8,128)}) %reduce-scatter.2.cloned.1.call-update) | async-done | bytes 262160 | tf_op jit(solution)/shard_map/reduce_scatter | solution.py:22
  102.6 1.6 convert_element_type.12
  104.2 0.0 all-gather.2.cloned.1.call-update
  104.2 0.0 copy-start.4
  104.2 0.0 all-reduce.3.cloned.1.call-start
  104.3 52.9 %all-gather.2.cloned.1.call-done = bf16[1024,1024]{1,0:T(8,128)(2,1)} async-done(((bf16[64,1024]{1,0:T(8,128)(2,1)}), bf16[1024,1024]{1,0:T(8,128)(2,1)}) %all-gather.2.cloned.1.call-update) | async-done | bytes 2097168 | tf_op jit(solution)/shard_map/all_gather | solution.py:28
  157.2 0.0 copy-start.3
  157.2 6.7 %fusion.9 = f32[1024,1024]{1,0:T(8,128)} fusion(bf16[1024,1024]{1,0:T(8,128)(2,1)} %all-gather.2.cloned.1.call-done), kind=kOutput, calls=%fused_computation.15 | convolution fusion | flops 2147483648 | bytes 6291456 | tf_op jit(solution)/shard_map/dot_general | solution.py:29
  163.9 0.0 copy-done.4
  163.9 0.0 copy-done.3
  163.9 2.6 convolution_bitcast_fusion
  166.5 0.0 all-reduce.3.cloned.1.call-update
  166.6 165.7 %all-reduce.3.cloned.1.call-done = (f32[1024,1024]{1,0:T(8,128)}, f32[512,1024]{0,1:T(8,128)}) async-done(((f32[1024,1024]{1,0:T(8,128)}, f32[512,1024]{0,1:T(8,128)}), (f32[1024,1024]{1,0:T(8,128)}, f32[512,1024]{0,1:T(8,128)})) %all-reduce.3.cloned.1.call-update) | async-done | bytes 6291472 | tf_op jit(solution)/shard_map/psum | solution.py:30
  332.3 0.0 copy-start.2
  332.3 3.0 fusion
  335.3 0.5 copy-done.2
  335.8 0.0 copy-start.1
  335.8 1.6 fusion.1
  337.3 0.0 copy-done.1
  337.3 1.5 fusion.2
  338.8 1.8 copy.3
  (1 shorter events, 0.0 us)
Async XLA Ops:
  6.5 1.2 copy-start
  6.5 96.0 %reduce-scatter.2.cloned.1.call-start = ((), (), s32[]{:S(2)}) async-start(), calls=%async_computation.1 | async-start | bytes 4456448 | tf_op jit(solution)/shard_map/reduce_scatter | solution.py:22
  12.2 145.0 %all-gather.2.cloned.1.call-start = ((), (), s32[]{:S(2)}) async-start(), calls=%async_computation.2 | async-start | bytes 2228224 | tf_op jit(solution)/shard_map/all_gather | solution.py:28
  104.2 59.7 %copy-start.4 = (bf16[1024,512]{1,0:T(8,128)(2,1)S(1)}, bf16[1024,512]{1,0:T(8,128)(2,1)}, u32[]{:S(2)}) copy-start(bf16[1024,512]{1,0:T(8,128)(2,1)} %param.2) | copy-start | bytes 3145732
  104.2 228.1 %all-reduce.3.cloned.1.call-start = ((), (), s32[]{:S(2)}) async-start(), calls=%async_computation.3 | async-start | bytes 12582912 | tf_op jit(solution)/shard_map/psum | solution.py:30
  157.2 6.7 %copy-start.3 = (bf16[1024,1024]{1,0:T(8,128)(2,1)S(1)}, bf16[1024,1024]{1,0:T(8,128)(2,1)}, u32[]{:S(2)}) copy-start(bf16[1024,1024]{1,0:T(8,128)(2,1)} %all-gather.2.cloned.1.call-done) | copy-start | bytes 6291460
  332.3 3.4 copy-start.2
  335.8 1.6 copy-start.1
Sparse Core Ops, SparseCore 0:
  12.3 90.2 reduce-scatter.1
  105.7 51.4 all-gather.1
  166.7 165.5 all-reduce.2
where the time goes:
time: 348 us; the launch traced here: 347 us
  waiting for transfers between devices  309 us (89%)
  matrix products  16.8 us (5%)
  between operations  13.1 us (4%)
  other arithmetic  4.61 us (1%)
  local copies, waits for them, and re-layouts  3.54 us (1%)
    psum x1, waiting for transfers between devices, body(): gram = lax.psum(partial_gram, 'sample') / total  166 us
    reduce_scatter x1, waiting for transfers between devices, body(): lax.psum_scatter(jnp.dot(features, panel, preferred_element_type=jnp.floa...  90.3 us
    all_gather x1, waiting for transfers between devices, body(): projected = lax.all_gather(share, 'feat', axis=0, tiled=True)  52.9 us
  transfers between devices with their start and end apart: 3, of which 3 were waited for; matrix products, arithmetic and copies ran while one was open for 0% of the time, Pallas kernels for 0%

commit v1 on v0

v1 whole, which is shorter than its diff:
```python
import math

import jax
import jax.numpy as jnp
from jax import lax
from jax.experimental import pallas as pl
from jax.experimental.pallas import tpu as pltpu
from jax.sharding import PartitionSpec as P

MESH = pl.DeviceIdType.MESH
F32, BF16 = jnp.float32, jnp.bfloat16
D = 8192
CHUNKS = 4
SKEW = 3
PER_CHUNK = 40
BLK = 32


def dot(a, b):
    return jnp.dot(a, b, preferred_element_type=F32)


def kernel(scale, f_hbm, v_hbm, out_hbm, fv, ft, fx, vv, vx, psum, l1, t2, l2, t3, l3, proj, projt, wf,
           hop1, hop1r, hop2, hop2r, hop4, hop4r, xs, xr, ob, send_sem, recv_sem, local_sem):
    s, f = lax.axis_index("sample"), lax.axis_index("feat")
    xl, z = s // 8, s % 8
    xh, y, core = f // 8, (f // 2) % 4, f % 2
    q = y // 2
    p = (y + q) % 2
    half = fv.shape[0] // 2
    width = fv.shape[1]
    cw = vv.shape[1] // CHUNKS

    def feat_dev(xh_, y_, core_):
        return (s, xh_ * 8 + y_ * 2 + core_)

    def sample_dev(xl_, z_):
        return (xl_ * 8 + z_, f)

    y_a = y + 1 - 2 * (y % 2)
    y_b = 3 - y
    sib = feat_dev(xh, y, 1 - core)
    dev_a, dev_b = feat_dev(xh, y_a, core), feat_dev(xh, y_b, core)
    dev_x = feat_dev(1 - xh, y, core)
    up, down = sample_dev(xl, (z + 1) % 8), sample_dev(xl, (z + 7) % 8)
    dev_l = sample_dev(1 - xl, z)

    loads = []
    loads.append(pltpu.make_async_copy(f_hbm, fv, local_sem.at[0]))
    loads.append(pltpu.make_async_copy(v_hbm, vv, local_sem.at[1]))
    for load in loads:
        load.start()

    barrier = pltpu.get_barrier_semaphore()
    for partner in (sib, dev_a, dev_b, dev_x, up, down, dev_l):
        pl.semaphore_signal(barrier, inc=1, device_id=partner, device_id_type=MESH)
    pl.semaphore_wait(barrier, 7)

    sent = []

    def send(index, src, dst, device):
        copy = pltpu.make_async_remote_copy(
            src_ref=src, dst_ref=dst, send_sem=send_sem.at[index], recv_sem=recv_sem.at[index],
            device_id=device, device_id_type=MESH,
        )
        copy.start()
        sent.append(copy)
        return copy

    base = CHUNKS * PER_CHUNK
    got_f = send(base, f_hbm.at[pl.ds(pl.multiple_of((1 - core) * half, half), half), :], fx, sib)
    got_v = [
        send(base + 1 + c, v_hbm.at[:, c * cw:(c + 1) * cw], vx.at[c], sib) for c in range(CHUNKS)
    ]
    state = {}

    def project(c):
        if c == 0:
            for load in loads:
                load.wait()
            got_f.wait_recv()
        got_v[c].wait_recv()
        own = fv[pl.ds(pl.multiple_of(core * half, half), half), :]
        total = dot(own, vv[:, c * cw:(c + 1) * cw]) + dot(fx[...], vx[c])
        psum[c] = total.reshape(16, BLK, cw)
        i = c * PER_CHUNK
        state[c, "a1"] = send(i, psum.at[c, pl.ds((1 - p) * 4, 4)], l1.at[c, 0], dev_a)
        state[c, "b1"] = send(i + 1, psum.at[c, pl.ds(8 + (1 - q) * 4, 4)], l1.at[c, 1], dev_b)
        if c == 0:
            ft[...] = fv[...].T

    def halve2(c):
        i = c * PER_CHUNK + 2
        state[c, "a1"].wait_recv()
        t2[c, 0] = psum[c, pl.ds(p * 4, 4)] + l1[c, 0]
        state[c, "a2"] = send(i, t2.at[c, 0, pl.ds((1 - q) * 2, 2)], l2.at[c, 0], dev_b)
        state[c, "b1"].wait_recv()
        t2[c, 1] = psum[c, pl.ds(8 + q * 4, 4)] + l1[c, 1]
        state[c, "b2"] = send(i + 1, t2.at[c, 1, pl.ds((1 - p) * 2, 2)], l2.at[c, 1], dev_a)

    def halve3(c):
        i = c * PER_CHUNK + 4
        state[c, "a2"].wait_recv()
        state[c, "b2"].wait_recv()
        t3[c, 1, 0] = t2[c, 0, q * 2 + 1 - xh] + l2[c, 0, 1 - xh]
        t3[c, 1, 1] = t2[c, 1, p * 2 + 1 - xh] + l2[c, 1, 1 - xh]
        state[c, "x3"] = send(i, t3.at[c, 1], l3.at[c], dev_x)
        t3[c, 0, 0] = t2[c, 0, q * 2 + xh] + l2[c, 0, xh]
        t3[c, 0, 1] = t2[c, 1, p * 2 + xh] + l2[c, 1, xh]

    mine = core * 16

    def blocks(c, at, n):
        return proj.at[c, pl.ds(at, n)]

    def share(c):
        i = c * PER_CHUNK + 5
        state[c, "x3"].wait_recv()
        done = (t3[c, 0] + l3[c]).astype(BF16)
        at_a = mine + p * 4 + q * 2 + xh
        at_b = mine + 8 + q * 4 + p * 2 + xh
        proj[c, at_a] = done[0]
        proj[c, at_b] = done[1]
        state[c, "xa"] = send(i, blocks(c, at_a, 1), blocks(c, at_a, 1), dev_x)
        state[c, "xb"] = send(i + 1, blocks(c, at_b, 1), blocks(c, at_b, 1), dev_x)

    def spread2(c):
        i = c * PER_CHUNK + 7
        state[c, "xa"].wait_recv()
        state[c, "xb"].wait_recv()
        a = blocks(c, mine + p * 4 + q * 2, 2)
        b = blocks(c, mine + 8 + q * 4 + p * 2, 2)
        state[c, "ga2"] = send(i, a, a, dev_b)
        state[c, "gb2"] = send(i + 1, b, b, dev_a)
        state[c, "sib"] = [send(i + 2, a, a, sib), send(i + 3, b, b, sib)]

    def spread4(c):
        i = c * PER_CHUNK + 11
        state[c, "ga2"].wait_recv()
        state[c, "gb2"].wait_recv()
        a = blocks(c, mine + p * 4, 4)
        b = blocks(c, mine + 8 + q * 4, 4)
        state[c, "ga4"] = send(i, a, a, dev_a)
        state[c, "gb4"] = send(i + 1, b, b, dev_b)
        a = blocks(c, mine + p * 4 + (1 - q) * 2, 2)
        b = blocks(c, mine + 8 + q * 4 + (1 - p) * 2, 2)
        state[c, "sib"] += [send(i + 2, a, a, sib), send(i + 3, b, b, sib)]

    def spread_core(c):
        i = c * PER_CHUNK + 15
        state[c, "ga4"].wait_recv()
        state[c, "gb4"].wait_recv()
        a = blocks(c, mine + (1 - p) * 4, 4)
        b = blocks(c, mine + 8 + (1 - q) * 4, 4)
        state[c, "sib"] += [send(i, a, a, sib), send(i + 1, b, b, sib)]

    def local_update(c):
        for copy in state[c, "sib"]:
            copy.wait_recv()
        pc = proj[c].reshape(1024, cw)
        projt[c * cw:(c + 1) * cw, :] = pc.T
        gram = dot(projt[0:(c + 1) * cw, :], pc)
        j = lax.broadcasted_iota(jnp.int32, gram.shape, 0)
        k = lax.broadcasted_iota(jnp.int32, gram.shape, 1) + c * cw
        upper = jnp.where(j <= k, gram, 0.0)
        high = upper.astype(BF16)
        low = (upper - high.astype(F32)).astype(BF16)
        rows = vv[:, 0:(c + 1) * cw]
        total = (dot(ft[...], pc) - (dot(rows, high) + dot(rows, low))) * scale
        wf[c] = total.reshape(8, 2, BLK, cw)
        i = c * PER_CHUNK + 17
        far = (z + 4) % 8
        hop1[c] = wf[c, far].astype(BF16)
        state[c, "u1"] = send(i, hop1.at[c, 0], hop1r.at[c, 0], up)
        state[c, "d1"] = send(i + 1, hop1.at[c, 1], hop1r.at[c, 1], down)

    def chain2(c):
        i = c * PER_CHUNK + 19
        state[c, "u1"].wait_recv()
        at = (z + 3) % 8
        hop2[c, 0, 0, 0] = (wf[c, at, 0] + hop1r[c, 0].astype(F32)).astype(BF16)
        hop2[c, 0, 0, 1] = wf[c, at, 1].astype(BF16)
        state[c, "u2"] = send(i, hop2.at[c, 0, 0], hop2r.at[c, 0, 0], up)
        state[c, "d1"].wait_recv()
        at = (z + 5) % 8
        hop2[c, 0, 1, 0] = wf[c, at, 0].astype(BF16)
        hop2[c, 0, 1, 1] = (wf[c, at, 1] + hop1r[c, 1].astype(F32)).astype(BF16)
        state[c, "d2"] = send(i + 1, hop2.at[c, 0, 1], hop2r.at[c, 0, 1], down)

    def chain3(c):
        i = c * PER_CHUNK + 21
        state[c, "u2"].wait_recv()
        hop2[c, 1, 0] = (wf[c, (z + 2) % 8] + hop2r[c, 0, 0].astype(F32)).astype(BF16)
        state[c, "u3"] = send(i, hop2.at[c, 1, 0], hop2r.at[c, 1, 0], up)
        state[c, "d2"].wait_recv()
        hop2[c, 1, 1] = (wf[c, (z + 6) % 8] + hop2r[c, 0, 1].astype(F32)).astype(BF16)
        state[c, "d3"] = send(i + 1, hop2.at[c, 1, 1], hop2r.at[c, 1, 1], down)

    def chain4(c):
        i = c * PER_CHUNK + 23
        state[c, "u3"].wait_recv()
        hop4[c, 0] = wf[c, (z + 1) % 8] + hop2r[c, 1, 0].astype(F32)
        state[c, "u4"] = send(i, hop4.at[c, 0], hop4r.at[c, 0], up)
        state[c, "d3"].wait_recv()
        hop4[c, 1] = wf[c, (z + 7) % 8] + hop2r[c, 1, 1].astype(F32)
        state[c, "d4"] = send(i + 1, hop4.at[c, 1], hop4r.at[c, 1], down)

    def chain_x(c):
        i = c * PER_CHUNK + 25
        state[c, "u4"].wait_recv()
        state[c, "d4"].wait_recv()
        xs[c, 0] = wf[c, z, 1 - xl] + hop4r[c, 0, 1 - xl] + hop4r[c, 1, 1 - xl]
        state[c, "xl"] = send(i, xs.at[c, 0], xr.at[c], dev_l)
        xs[c, 1] = wf[c, z, xl] + hop4r[c, 0, xl] + hop4r[c, 1, xl]

    def finish(c):
        i = c * PER_CHUNK + 26
        state[c, "xl"].wait_recv()
        at = z * 2 + xl
        ob[c, at] = (xs[c, 1] + xr[c]).astype(BF16)
        state[c, "o0"] = send(i, ob.at[c, at], ob.at[c, at], dev_l)

    def ring(c, hop, at_up, at_down, n):
        i = c * PER_CHUNK + 27 + 2 * hop
        a, b = ob.at[c, pl.ds(at_up, n)], ob.at[c, pl.ds(at_down, n)]
        state[c, "up", hop] = send(i, a, a, up)
        state[c, "down", hop] = send(i + 1, b, b, down)

    def ring_wait(c, hop):
        state[c, "up", hop].wait_recv()
        state[c, "down", hop].wait_recv()

    def ring1(c):
        state[c, "o0"].wait_recv()
        ring(c, 0, z * 2, z * 2, 2)

    def ring2(c):
        ring_wait(c, 0)
        ring(c, 1, ((z + 7) % 8) * 2, ((z + 1) % 8) * 2, 2)

    def ring3(c):
        ring_wait(c, 1)
        ring(c, 2, ((z + 6) % 8) * 2, ((z + 2) % 8) * 2, 2)

    def ring4(c):
        ring_wait(c, 2)
        ring(c, 3, ((z + 5) % 8) * 2, ((z + 3) % 8) * 2 + 1, 1)

    def write(c):
        ring_wait(c, 3)
        copy = pltpu.make_async_copy(ob.at[c], out_hbm.at[:, :, c * cw:(c + 1) * cw], local_sem.at[2 + c])
        copy.start()
        state[c, "out"] = copy

    stages = [project, halve2, halve3, share, spread2, spread4, spread_core, local_update, chain2, chain3,
              chain4, chain_x, finish, ring1, ring2, ring3, ring4, write]
    for tick in range(len(stages) + SKEW * (CHUNKS - 1)):
        for c in range(CHUNKS):
            at = tick - SKEW * c
            if 0 <= at < len(stages):
                stages[at](c)
    for copy in sent:
        copy.wait_send()
    for c in range(CHUNKS):
        state[c, "out"].wait()


def body(features, panel):
    rows, width = features.shape
    k = panel.shape[1]
    cw = k // CHUNKS
    n = CHUNKS
    scale = math.sqrt(D) / (rows * lax.axis_size("sample"))
    scratch = [
        pltpu.VMEM((rows, width), BF16),
        pltpu.VMEM((width, rows), BF16),
        pltpu.VMEM((rows // 2, width), BF16),
        pltpu.VMEM((width, k), BF16),
        pltpu.VMEM((n, width, cw), BF16),
        pltpu.VMEM((n, 16, BLK, cw), F32),
        pltpu.VMEM((n, 2, 4, BLK, cw), F32),
        pltpu.VMEM((n, 2, 4, BLK, cw), F32),
        pltpu.VMEM((n, 2, 2, BLK, cw), F32),
        pltpu.VMEM((n, 2, 2, BLK, cw), F32),
        pltpu.VMEM((n, 2, BLK, cw), F32),
        pltpu.VMEM((n, 32, BLK, cw), BF16),
        pltpu.VMEM((k, rows), BF16),
        pltpu.VMEM((n, 8, 2, BLK, cw), F32),
        pltpu.VMEM((n, 2, BLK, cw), BF16),
        pltpu.VMEM((n, 2, BLK, cw), BF16),
        pltpu.VMEM((n, 2, 2, 2, BLK, cw), BF16),
        pltpu.VMEM((n, 2, 2, 2, BLK, cw), BF16),
        pltpu.VMEM((n, 2, 2, BLK, cw), F32),
        pltpu.VMEM((n, 2, 2, BLK, cw), F32),
        pltpu.VMEM((n, 2, BLK, cw), F32),
        pltpu.VMEM((n, BLK, cw), F32),
        pltpu.VMEM((n, 16, BLK, cw), BF16),
        pltpu.SemaphoreType.DMA((n * PER_CHUNK + 1 + n,)),
        pltpu.SemaphoreType.DMA((n * PER_CHUNK + 1 + n,)),
        pltpu.SemaphoreType.DMA((2 + n,)),
    ]
    out = pl.pallas_call(
        lambda *refs: kernel(scale, *refs),
        out_shape=jax.ShapeDtypeStruct((16, BLK, k), BF16),
        in_specs=[pl.BlockSpec(memory_space=pl.ANY)] * 2,
        out_specs=pl.BlockSpec(memory_space=pl.ANY),
        scratch_shapes=scratch,
        compiler_params=pltpu.CompilerParams(
            collective_id=0, has_side_effects=True, vmem_limit_bytes=60 * 2**20
        ),
        cost_estimate=pl.CostEstimate(flops=6 * 10**9, bytes_accessed=4 * 2**20, transcendentals=0),
        name="update",
    )(features, panel)
    return out.reshape(width, k).astype(F32)


def solution(mesh):
    return jax.shard_map(
        body,
        mesh=mesh,
        in_specs=(P("sample", "feat"), P("feat", None)),
        out_specs=P("feat", None),
        check_vma=False,
    )
```

time: 348 us -> 116 us (0.33)
  waiting for transfers between devices: 309 us -> 0 us
  Pallas kernels: 0 us -> 113 us
  matrix products: 16.8 us -> 0 us
  between operations: 13.1 us -> 0.01 us
  local copies, waits for them, and re-layouts: 3.54 us -> 0 us
    psum x1 -> x0, waiting for transfers between devices: 166 us -> none  [body(): gram = lax.psum(partial_gram, 'sample') / total]
    pallas_call x0 -> x1, Pallas kernels: none -> 113 us  [body(): pl.pallas_call(lambda *refs: kernel(scale, *refs), out_shape=jax.ShapeDty...]
    reduce_scatter x1 -> x0, waiting for transfers between devices: 90.3 us -> none  [body(): lax.psum_scatter(jnp.dot(features, panel, preferred_element_type=jnp.floa...]
    all_gather x1 -> x0, waiting for transfers between devices: 52.9 us -> none  [body(): projected = lax.all_gather(share, 'feat', axis=0, tiled=True)]
    dot_general x5 -> x0, matrix products: 16.8 us -> none  [the longest x1 6.7 us: body(): jnp.dot(projected.T, projected, preferred_element_type=jnp.float32)]
  transfers between devices with their start and end apart: 3 -> 0, of which waited for: 3 -> 0; matrix products, arithmetic and copies ran while one was open for 0% -> 0% of each run, Pallas kernels for 0% -> 0%
where the time goes in v1:
time: 116 us
  Pallas kernels  113 us (97%)
  other arithmetic  2.79 us (2%)
    pallas_call x1, Pallas kernels, body(): pl.pallas_call(lambda *refs: kernel(scale, *refs), out_shape=jax.ShapeDty...  113 us
    convert_element_type x1, other arithmetic, body(): return out.reshape(width, k).astype(F32)  2.79 us

profile of v1, /device:TPU:2, one launch (start us, length us, event | category | flops | bytes accessed | tf_op | source)
XLA Modules:
  0.0 115.9 jit_solution(11903471342846065305)
XLA Ops:
  0.0 113.1 %update.1 = bf16[16,32,1024]{2,1,0:T(8,128)(2,1)} custom-call(bf16[1024,512]{1,0:T(8,128)(2,1)} %refs_0_.1, bf16[512,1024]{1,0:T(8,128)(2,1)} %refs_1_.1), custom_call_target="tpu_custom_call" | custom-call | flops 6000000000 | bytes 4194304 | tf_op jit(solution)/shard_map/update/pallas_call | solution.py:302
  113.1 2.8 %bitcast_convert_fusion = f32[512,1024]{1,0:T(8,128)} fusion(bf16[16,32,1024]{2,1,0:T(8,128)(2,1)} %update.1), kind=kLoop, calls=%fused_computation | loop fusion | flops 524288 | bytes 3145728 | tf_op jit(solution)/shard_map/convert_element_type | solution.py:314

commit v2 on v1

v2 whole, which is shorter than its diff:
```python
import math

import jax
import jax.numpy as jnp
from jax import lax
from jax.experimental import pallas as pl
from jax.experimental.pallas import tpu as pltpu
from jax.sharding import PartitionSpec as P

MESH = pl.DeviceIdType.MESH
F32, BF16 = jnp.float32, jnp.bfloat16
D = 8192
CHUNKS = 4
PER_CHUNK = 45
ORDER = (
    0, 1, 2, 3, 0, 1, 2, 3, 0, 1, 2, 3, 0, 1, 2, 0, 3, 0, 1, 2, 1, 2,
    3, 0, 3, 1, 2, 0, 3, 1, 2, 0, 3, 1, 2, 0, 3, 1, 2, 0, 3, 1, 2, 3,
)
BLK = 32


def dot(a, b):
    return jnp.dot(a, b, preferred_element_type=F32)


def kernel(scale, f_hbm, v_hbm, out_hbm, fv, ft, fx, vv, vx, psum, l1, t2, l2, proj, projt, wf,
           half_out, half_in, zs_out, zs_in, ob, send_sem, recv_sem, local_sem):
    s, f = lax.axis_index("sample"), lax.axis_index("feat")
    xl, z = s // 8, s % 8
    xh, y, core = f // 8, (f // 2) % 4, f % 2
    q = y // 2
    p = (y + q) % 2
    half = fv.shape[0] // 2
    width = fv.shape[1]
    cw = vv.shape[1] // CHUNKS

    def feat_dev(xh_, y_, core_):
        return (s, xh_ * 8 + y_ * 2 + core_)

    def sample_dev(xl_, z_):
        return (xl_ * 8 + z_, f)

    y_a = y + 1 - 2 * (y % 2)
    y_b = 3 - y
    sib = feat_dev(xh, y, 1 - core)
    dev_a, dev_b = feat_dev(xh, y_a, core), feat_dev(xh, y_b, core)
    dev_x = feat_dev(1 - xh, y, core)
    dev_l = sample_dev(1 - xl, z)
    dev_ax, dev_bx = feat_dev(1 - xh, y_a, core), feat_dev(1 - xh, y_b, core)
    ring = {k: sample_dev(xl, (z + k) % 8) for k in range(1, 8)}

    loads = []
    loads.append(pltpu.make_async_copy(f_hbm, fv, local_sem.at[0]))
    loads.append(pltpu.make_async_copy(v_hbm, vv, local_sem.at[1]))
    for load in loads:
        load.start()

    barrier = pltpu.get_barrier_semaphore()
    for partner in (sib, dev_a, dev_b, dev_x, dev_ax, dev_bx, dev_l, *ring.values()):
        pl.semaphore_signal(barrier, inc=1, device_id=partner, device_id_type=MESH)
    pl.semaphore_wait(barrier, 14)

    sent = []

    def send(index, src, dst, device):
        copy = pltpu.make_async_remote_copy(
            src_ref=src, dst_ref=dst, send_sem=send_sem.at[index], recv_sem=recv_sem.at[index],
            device_id=device, device_id_type=MESH,
        )
        copy.start()
        sent.append(copy)
        return copy

    base = CHUNKS * PER_CHUNK
    got_f = send(base, f_hbm.at[pl.ds(pl.multiple_of((1 - core) * half, half), half), :], fx, sib)
    got_v = [
        send(base + 1 + c, v_hbm.at[:, c * cw:(c + 1) * cw], vx.at[c], sib) for c in range(CHUNKS)
    ]
    state = {}

    def project(c):
        if c == 0:
            for load in loads:
                load.wait()
            got_f.wait_recv()
        got_v[c].wait_recv()
        own = fv[pl.ds(pl.multiple_of(core * half, half), half), :]
        total = dot(own, vv[:, c * cw:(c + 1) * cw]) + dot(fx[...], vx[c])
        psum[c] = total.reshape(16, BLK, cw)
        i = c * PER_CHUNK
        state[c, "a1"] = send(i, psum.at[c, pl.ds((1 - p) * 4, 4)], l1.at[c, 0], dev_a)
        state[c, "b1"] = send(i + 1, psum.at[c, pl.ds(8 + (1 - q) * 4, 4)], l1.at[c, 1], dev_b)
        if c == 0:
            ft[...] = fv[...].T

    def halve2(c):
        i = c * PER_CHUNK + 2
        state[c, "a1"].wait_recv()
        t2[c, 0] = psum[c, pl.ds(p * 4, 4)] + l1[c, 0]
        at, flip = (q * 2, (1 - q) * 2)
        state[c, "r2"] = [
            send(i, t2.at[c, 0, flip + 1 - xh], l2.at[c, 0, 0], dev_bx),
            send(i + 1, t2.at[c, 0, at + 1 - xh], l2.at[c, 0, 1], dev_x),
            send(i + 2, t2.at[c, 0, flip + xh], l2.at[c, 0, 2], dev_b),
        ]
        state[c, "b1"].wait_recv()
        t2[c, 1] = psum[c, pl.ds(8 + q * 4, 4)] + l1[c, 1]
        at, flip = (p * 2, (1 - p) * 2)
        state[c, "r2"] += [
            send(i + 3, t2.at[c, 1, flip + 1 - xh], l2.at[c, 1, 0], dev_ax),
            send(i + 4, t2.at[c, 1, at + 1 - xh], l2.at[c, 1, 1], dev_x),
            send(i + 5, t2.at[c, 1, flip + xh], l2.at[c, 1, 2], dev_a),
        ]

    mine = core * 16

    def blocks(c, at, n):
        return proj.at[c, pl.ds(at, n)]

    def share(c):
        i = c * PER_CHUNK + 8
        for copy in state[c, "r2"]:
            copy.wait_recv()
        at_a = mine + p * 4 + q * 2 + xh
        at_b = mine + 8 + q * 4 + p * 2 + xh
        proj[c, at_a] = (t2[c, 0, q * 2 + xh] + l2[c, 0, 0] + l2[c, 0, 1] + l2[c, 0, 2]).astype(BF16)
        a = proj.at[c, at_a]
        state[c, "g2"] = [send(i, a, a, dev_bx), send(i + 1, a, a, dev_x), send(i + 2, a, a, dev_b)]
        proj[c, at_b] = (t2[c, 1, p * 2 + xh] + l2[c, 1, 0] + l2[c, 1, 1] + l2[c, 1, 2]).astype(BF16)
        b = proj.at[c, at_b]
        state[c, "g2"] += [send(i + 3, b, b, dev_ax), send(i + 4, b, b, dev_x), send(i + 5, b, b, dev_a)]

    def spread4(c):
        i = c * PER_CHUNK + 14
        for copy in state[c, "g2"]:
            copy.wait_recv()
        a = blocks(c, mine + p * 4, 4)
        b = blocks(c, mine + 8 + q * 4, 4)
        state[c, "ga4"] = send(i, a, a, dev_a)
        state[c, "gb4"] = send(i + 1, b, b, dev_b)
        state[c, "sib"] = [send(i + 2, a, a, sib), send(i + 3, b, b, sib)]

    def spread_core(c):
        i = c * PER_CHUNK + 18
        state[c, "ga4"].wait_recv()
        state[c, "gb4"].wait_recv()
        a = blocks(c, mine + (1 - p) * 4, 4)
        b = blocks(c, mine + 8 + (1 - q) * 4, 4)
        state[c, "sib"] += [send(i, a, a, sib), send(i + 1, b, b, sib)]

    def local_update(c):
        for copy in state[c, "sib"]:
            copy.wait_recv()
        pc = proj[c].reshape(1024, cw)
        projt[c * cw:(c + 1) * cw, :] = pc.T
        gram = dot(projt[0:(c + 1) * cw, :], pc)
        j = lax.broadcasted_iota(jnp.int32, gram.shape, 0)
        k = lax.broadcasted_iota(jnp.int32, gram.shape, 1) + c * cw
        upper = jnp.where(j <= k, gram, 0.0)
        high = upper.astype(BF16)
        low = (upper - high.astype(F32)).astype(BF16)
        rows = vv[:, 0:(c + 1) * cw]
        total = (dot(ft[...], pc) - (dot(rows, high) + dot(rows, low))) * scale
        wf[c] = total.reshape(2, 8, BLK, cw)
        half_out[c] = wf[c, 1 - xl].astype(BF16)
        state[c, "xl"] = send(c * PER_CHUNK + 20, half_out.at[c], half_in.at[c], dev_l)

    def scatter(c):
        i = c * PER_CHUNK + 21
        state[c, "xl"].wait_recv()
        both = wf[c, xl] + half_in[c].astype(F32)
        wf[c, xl] = both
        zs_out[c] = both.astype(BF16)
        state[c, "zs"] = [
            send(i + k, zs_out.at[c, (z + k) % 8], zs_in.at[c, k - 1], ring[k]) for k in (4, 3, 5, 2, 6, 1, 7)
        ]

    def finish(c):
        i = c * PER_CHUNK + 29
        for copy in state[c, "zs"]:
            copy.wait_recv()
        total = wf[c, xl, z]
        for k in range(7):
            total = total + zs_in[c, k].astype(F32)
        at = xl * 8 + z
        ob[c, at] = total.astype(BF16)
        a = ob.at[c, at]
        state[c, "o1"] = [send(i + n, a, a, ring[k]) for n, k in enumerate((2, 6, 1, 7))]
        state[c, "ox"] = [send(i + 4, a, a, dev_l)]

    def own(c, k):
        return ob.at[c, xl * 8 + (z + k) % 8]

    def gather2(c):
        i = c * PER_CHUNK + 34
        up2, down2, up1, down1 = state[c, "o1"]
        down1.wait_recv()
        up2.wait_recv()
        a, b = own(c, 1), own(c, 6)
        state[c, "o2"] = [send(i, a, a, ring[6])]
        b2 = b.at[pl.ds(0, BLK // 2)]
        state[c, "o2"] += [send(i + 1, b2, b2, ring[2])]
        up1.wait_recv()
        down2.wait_recv()
        a, b = own(c, 7), own(c, 2)
        state[c, "o2"] += [send(i + 2, a, a, ring[2])]
        b2 = b.at[pl.ds(BLK // 2, BLK // 2)]
        state[c, "o2"] += [send(i + 3, b2, b2, ring[6])]
        for n, k in enumerate((1, 7, 2, 6)):
            a = own(c, k)
            state[c, "ox"] += [send(i + 4 + n, a, a, dev_l)]

    def swap(c):
        i = c * PER_CHUNK + 42
        for copy in state[c, "o2"]:
            copy.wait_recv()
        for n, k in enumerate((3, 4, 5)):
            a = own(c, k)
            state[c, "ox"] += [send(i + n, a, a, dev_l)]

    def write(c):
        for copy in state[c, "ox"]:
            copy.wait_recv()
        copy = pltpu.make_async_copy(ob.at[c], out_hbm.at[:, :, c * cw:(c + 1) * cw], local_sem.at[2 + c])
        copy.start()
        state[c, "out"] = copy

    stages = [project, halve2, share, spread4, spread_core, local_update, scatter, finish, gather2, swap, write]
    done = [0] * CHUNKS
    for c in ORDER:
        stages[done[c]](c)
        done[c] += 1
    for copy in sent:
        copy.wait_send()
    for c in range(CHUNKS):
        state[c, "out"].wait()


def body(features, panel):
    rows, width = features.shape
    k = panel.shape[1]
    cw = k // CHUNKS
    n = CHUNKS
    scale = math.sqrt(D) / (rows * lax.axis_size("sample"))
    scratch = [
        pltpu.VMEM((rows, width), BF16),
        pltpu.VMEM((width, rows), BF16),
        pltpu.VMEM((rows // 2, width), BF16),
        pltpu.VMEM((width, k), BF16),
        pltpu.VMEM((n, width, cw), BF16),
        pltpu.VMEM((n, 16, BLK, cw), F32),
        pltpu.VMEM((n, 2, 4, BLK, cw), F32),
        pltpu.VMEM((n, 2, 4, BLK, cw), F32),
        pltpu.VMEM((n, 2, 3, BLK, cw), F32),
        pltpu.VMEM((n, 32, BLK, cw), BF16),
        pltpu.VMEM((k, rows), BF16),
        pltpu.VMEM((n, 2, 8, BLK, cw), F32),
        pltpu.VMEM((n, 8, BLK, cw), BF16),
        pltpu.VMEM((n, 8, BLK, cw), BF16),
        pltpu.VMEM((n, 8, BLK, cw), BF16),
        pltpu.VMEM((n, 7, BLK, cw), BF16),
        pltpu.VMEM((n, 16, BLK, cw), BF16),
        pltpu.SemaphoreType.DMA((n * PER_CHUNK + 1 + n,)),
        pltpu.SemaphoreType.DMA((n * PER_CHUNK + 1 + n,)),
        pltpu.SemaphoreType.DMA((2 + n,)),
    ]
    out = pl.pallas_call(
        lambda *refs: kernel(scale, *refs),
        out_shape=jax.ShapeDtypeStruct((16, BLK, k), BF16),
        in_specs=[pl.BlockSpec(memory_space=pl.ANY)] * 2,
        out_specs=pl.BlockSpec(memory_space=pl.ANY),
        scratch_shapes=scratch,
        compiler_params=pltpu.CompilerParams(
            collective_id=0, has_side_effects=True, vmem_limit_bytes=60 * 2**20
        ),
        cost_estimate=pl.CostEstimate(flops=6 * 10**9, bytes_accessed=4 * 2**20, transcendentals=0),
        name="update",
    )(features, panel)
    return out.reshape(width, k).astype(F32)


def solution(mesh):
    return jax.shard_map(
        body,
        mesh=mesh,
        in_specs=(P("sample", "feat"), P("feat", None)),
        out_specs=P("feat", None),
        check_vma=False,
    )
```

time: 116 us -> 79.2 us (0.68)
  Pallas kernels: 113 us -> 76.3 us
    pallas_call x1, Pallas kernels: 113 us -> 76.3 us  [body(): pl.pallas_call(lambda *refs: kernel(scale, *refs), out_shape=jax.ShapeDty...]
where the time goes in v2:
time: 79.2 us; the launch traced here: 79.1 us
  Pallas kernels  76.3 us (96%)
  other arithmetic  2.79 us (4%)
    pallas_call x1, Pallas kernels, body(): pl.pallas_call(lambda *refs: kernel(scale, *refs), out_shape=jax.ShapeDty...  76.3 us
    convert_element_type x1, other arithmetic, body(): return out.reshape(width, k).astype(F32)  2.79 us

profile of v2, /device:TPU:2, one launch (start us, length us, event | category | flops | bytes accessed | tf_op | source)
XLA Modules:
  0.0 79.1 jit_solution(1888974933998851425)
XLA Ops:
  0.0 76.3 %update.1 = bf16[16,32,1024]{2,1,0:T(8,128)(2,1)} custom-call(bf16[1024,512]{1,0:T(8,128)(2,1)} %refs_0_.1, bf16[512,1024]{1,0:T(8,128)(2,1)} %refs_1_.1), custom_call_target="tpu_custom_call" | custom-call | flops 6000000000 | bytes 4194304 | tf_op jit(solution)/shard_map/update/pallas_call | solution.py:267
  76.3 2.8 %bitcast_convert_fusion = f32[512,1024]{1,0:T(8,128)} fusion(bf16[16,32,1024]{2,1,0:T(8,128)(2,1)} %update.1), kind=kLoop, calls=%fused_computation | loop fusion | flops 524288 | bytes 3145728 | tf_op jit(solution)/shard_map/convert_element_type | solution.py:279

commit v3 on v2

v3 whole, which is shorter than its diff:
```python
import math

import jax
import jax.numpy as jnp
from jax import lax
from jax.experimental import pallas as pl
from jax.experimental.pallas import tpu as pltpu
from jax.sharding import PartitionSpec as P

MESH = pl.DeviceIdType.MESH
F32, BF16 = jnp.float32, jnp.bfloat16
D = 8192
CHUNKS = 4
PER_CHUNK = 45
TURN = 3
ORDER = (
    0, 1, 0, 1, 2, 0, 2, 3, 1, 0, 3, 2, 0, 1, 3, 2, 0, 1, 0, 3, 1, 2, 1, 0,
    2, 3, 2, 3, 1, 0, 3, 2, 0, 3, 1, 2, 0, 3, 0, 1, 2, 3, 1, 2, 3, 1, 2, 3,
)
BLK = 32


def dot(a, b):
    return jnp.dot(a, b, preferred_element_type=F32)


def kernel(scale, f_hbm, v_hbm, out_hbm, fv, ft, vv, part, part_in, psum, l1, t2, l2, proj, projt, wf,
           half_out, half_in, zs_out, zs_in, ob, send_sem, recv_sem, local_sem):
    s, f = lax.axis_index("sample"), lax.axis_index("feat")
    xl, z = s // 8, s % 8
    xh, y, core = f // 8, (f // 2) % 4, f % 2
    q = y // 2
    p = (y + q) % 2
    half = fv.shape[1] // 2
    cw = vv.shape[1] // CHUNKS

    def feat_dev(xh_, y_, core_):
        return (s, xh_ * 8 + y_ * 2 + core_)

    def sample_dev(xl_, z_):
        return (xl_ * 8 + z_, f)

    y_a = y + 1 - 2 * (y % 2)
    y_b = 3 - y
    sib = feat_dev(xh, y, 1 - core)
    dev_a, dev_b = feat_dev(xh, y_a, core), feat_dev(xh, y_b, core)
    dev_x = feat_dev(1 - xh, y, core)
    dev_l = sample_dev(1 - xl, z)
    dev_ax, dev_bx = feat_dev(1 - xh, y_a, core), feat_dev(1 - xh, y_b, core)
    ring = {k: sample_dev(xl, (z + k) % 8) for k in range(1, 8)}

    loads = [pltpu.make_async_copy(v_hbm, vv, local_sem.at[0]), pltpu.make_async_copy(f_hbm, fv, local_sem.at[1])]
    for load in loads:
        load.start()

    barrier = pltpu.get_barrier_semaphore()
    for partner in (sib, dev_a, dev_b, dev_x, dev_ax, dev_bx, dev_l, *ring.values()):
        pl.semaphore_signal(barrier, inc=1, device_id=partner, device_id_type=MESH)
    for load in loads:
        load.wait()

    def partial(c, side):
        rows = fv[pl.ds(pl.multiple_of(side * BLK * 16, BLK * 16), BLK * 16), :]
        return dot(rows, vv[:, c * cw:(c + 1) * cw]).reshape(16, BLK, cw)

    pl.semaphore_wait(barrier, 14)

    sent = []

    def send(index, src, dst, device):
        copy = pltpu.make_async_remote_copy(
            src_ref=src, dst_ref=dst, send_sem=send_sem.at[index], recv_sem=recv_sem.at[index],
            device_id=device, device_id_type=MESH,
        )
        copy.start()
        sent.append(copy)
        return copy

    state = {}

    def project(c):
        part[c] = partial(c, 1 - core)
        state[c, "half"] = send(c * PER_CHUNK, part.at[c], part_in.at[c], sib)
        psum[c] = partial(c, core)

    def fold(c):
        i = c * PER_CHUNK + 1
        state[c, "half"].wait_recv()
        at = pl.ds((1 - p) * 4, 4)
        psum[c, at] = psum[c, at] + part_in[c, at]
        state[c, "a1"] = send(i, psum.at[c, at], l1.at[c, 0], dev_a)
        at = pl.ds(8 + (1 - q) * 4, 4)
        psum[c, at] = psum[c, at] + part_in[c, at]
        state[c, "b1"] = send(i + 1, psum.at[c, at], l1.at[c, 1], dev_b)
        for at in (pl.ds(p * 4, 4), pl.ds(8 + q * 4, 4)):
            psum[c, at] = psum[c, at] + part_in[c, at]
        if c == TURN:
            ft[...] = fv[...].T

    def halve2(c):
        i = c * PER_CHUNK + 3
        state[c, "a1"].wait_recv()
        for slot, at in enumerate((q * 2 + 1 - xh, (1 - q) * 2 + 1 - xh, (1 - q) * 2 + xh, q * 2 + xh)):
            t2[c, 2 * slot] = psum[c, p * 4 + at] + l1[c, 0, at]
        copies = [
            send(i, t2.at[c, 2], l2.at[c, 2], dev_bx),
            send(i + 1, t2.at[c, 4], l2.at[c, 4], dev_b),
        ]
        state[c, "b1"].wait_recv()
        for slot, at in enumerate((p * 2 + 1 - xh, (1 - p) * 2 + 1 - xh, (1 - p) * 2 + xh, p * 2 + xh)):
            t2[c, 2 * slot + 1] = psum[c, 8 + q * 4 + at] + l1[c, 1, at]
        copies += [
            send(i + 2, t2.at[c, 3], l2.at[c, 3], dev_ax),
            send(i + 3, t2.at[c, pl.ds(0, 2)], l2.at[c, pl.ds(0, 2)], dev_x),
            send(i + 4, t2.at[c, 5], l2.at[c, 5], dev_a),
        ]
        state[c, "r2"] = copies

    def share(c):
        i = c * PER_CHUNK + 8
        for copy in state[c, "r2"]:
            copy.wait_recv()
        total = (t2[c, 6:8] + l2[c, 0:2] + l2[c, 2:4] + l2[c, 4:6]).astype(BF16)
        at_a = p * 4 + q * 2 + xh
        at_b = 8 + q * 4 + p * 2 + xh
        proj[c, core, at_a] = total[0]
        proj[c, core, at_b] = total[1]
        a, b = proj.at[c, core, at_a], proj.at[c, core, at_b]
        state[c, "g2"] = [
            send(i, a, a, dev_bx),
            send(i + 1, b, b, dev_ax),
            send(i + 2, a, a, dev_x),
            send(i + 3, b, b, dev_x),
            send(i + 4, a, a, dev_b),
            send(i + 5, b, b, dev_a),
        ]

    def spread4(c):
        i = c * PER_CHUNK + 14
        for copy in state[c, "g2"]:
            copy.wait_recv()
        a = proj.at[c, core, pl.ds(p * 4, 4)]
        b = proj.at[c, core, pl.ds(8 + q * 4, 4)]
        state[c, "g4"] = [send(i, a, a, dev_a), send(i + 1, b, b, dev_b)]

    def spread_core(c):
        for copy in state[c, "g4"]:
            copy.wait_recv()
        a = proj.at[c, core]
        state[c, "sib"] = send(c * PER_CHUNK + 16, a, a, sib)

    def local_update(c):
        state[c, "sib"].wait_recv()
        pc = proj[c].reshape(1024, cw)
        projt[c * cw:(c + 1) * cw, :] = pc.T
        gram = dot(projt[0:(c + 1) * cw, :], pc)
        j = lax.broadcasted_iota(jnp.int32, gram.shape, 0)
        k = lax.broadcasted_iota(jnp.int32, gram.shape, 1) + c * cw
        upper = jnp.where(j <= k, gram, 0.0)
        high = upper.astype(BF16)
        low = (upper - high.astype(F32)).astype(BF16)

        def rows_of(side):
            at = pl.ds(pl.multiple_of(side * half, half), half)
            rows = vv[at, 0:(c + 1) * cw]
            total = (dot(ft[at, :], pc) - (dot(rows, high) + dot(rows, low))) * scale
            return total.reshape(8, BLK, cw)

        half_out[c] = rows_of(1 - xl).astype(BF16)
        state[c, "xl"] = send(c * PER_CHUNK + 20, half_out.at[c], half_in.at[c], dev_l)
        wf[c] = rows_of(xl)

    def scatter(c):
        i = c * PER_CHUNK + 21
        state[c, "xl"].wait_recv()
        both = wf[c] + half_in[c].astype(F32)
        wf[c] = both
        zs_out[c] = both.astype(BF16)
        state[c, "zs"] = [
            send(i + k, zs_out.at[c, (z + k) % 8], zs_in.at[c, k - 1], ring[k]) for k in (4, 3, 5, 2, 6, 1, 7)
        ]

    def finish(c):
        i = c * PER_CHUNK + 29
        for copy in state[c, "zs"]:
            copy.wait_recv()
        total = wf[c, z]
        for k in range(7):
            total = total + zs_in[c, k].astype(F32)
        at = xl * 8 + z
        ob[c, at] = total.astype(BF16)
        a = ob.at[c, at]
        state[c, "o1"] = [send(i + n, a, a, ring[k]) for n, k in enumerate((2, 6, 1, 7))]
        state[c, "ox"] = [send(i + 4, a, a, dev_l)]

    def own(c, k):
        return ob.at[c, xl * 8 + (z + k) % 8]

    def gather2(c):
        i = c * PER_CHUNK + 34
        up2, down2, up1, down1 = state[c, "o1"]
        down1.wait_recv()
        up2.wait_recv()
        a, b = own(c, 1), own(c, 6)
        state[c, "o2"] = [send(i, a, a, ring[6])]
        b2 = b.at[pl.ds(0, BLK // 2)]
        state[c, "o2"] += [send(i + 1, b2, b2, ring[2])]
        up1.wait_recv()
        down2.wait_recv()
        a, b = own(c, 7), own(c, 2)
        state[c, "o2"] += [send(i + 2, a, a, ring[2])]
        b2 = b.at[pl.ds(BLK // 2, BLK // 2)]
        state[c, "o2"] += [send(i + 3, b2, b2, ring[6])]
        for n, k in enumerate((1, 7, 2, 6)):
            a = own(c, k)
            state[c, "ox"] += [send(i + 4 + n, a, a, dev_l)]

    def swap(c):
        i = c * PER_CHUNK + 42
        for copy in state[c, "o2"]:
            copy.wait_recv()
        for n, k in enumerate((3, 4, 5)):
            a = own(c, k)
            state[c, "ox"] += [send(i + n, a, a, dev_l)]

    def write(c):
        for copy in state[c, "ox"]:
            copy.wait_recv()
        copy = pltpu.make_async_copy(ob.at[c], out_hbm.at[:, :, c * cw:(c + 1) * cw], local_sem.at[2 + c])
        copy.start()
        state[c, "out"] = copy

    stages = [project, fold, halve2, share, spread4, spread_core, local_update, scatter, finish, gather2, swap, write]
    done = [0] * CHUNKS
    for c in ORDER:
        stages[done[c]](c)
        done[c] += 1
    for copy in sent:
        copy.wait_send()
    for c in range(CHUNKS):
        state[c, "out"].wait()


def body(features, panel):
    rows, width = features.shape
    k = panel.shape[1]
    cw = k // CHUNKS
    n = CHUNKS
    scale = math.sqrt(D) / (rows * lax.axis_size("sample"))
    scratch = [
        pltpu.VMEM((rows, width), BF16),
        pltpu.VMEM((width, rows), BF16),
        pltpu.VMEM((width, k), BF16),
        pltpu.VMEM((n, 16, BLK, cw), F32),
        pltpu.VMEM((n, 16, BLK, cw), F32),
        pltpu.VMEM((n, 16, BLK, cw), F32),
        pltpu.VMEM((n, 2, 4, BLK, cw), F32),
        pltpu.VMEM((n, 8, BLK, cw), F32),
        pltpu.VMEM((n, 6, BLK, cw), F32),
        pltpu.VMEM((n, 2, 16, BLK, cw), BF16),
        pltpu.VMEM((k, rows), BF16),
        pltpu.VMEM((n, 8, BLK, cw), F32),
        pltpu.VMEM((n, 8, BLK, cw), BF16),
        pltpu.VMEM((n, 8, BLK, cw), BF16),
        pltpu.VMEM((n, 8, BLK, cw), BF16),
        pltpu.VMEM((n, 7, BLK, cw), BF16),
        pltpu.VMEM((n, 16, BLK, cw), BF16),
        pltpu.SemaphoreType.DMA((n * PER_CHUNK,)),
        pltpu.SemaphoreType.DMA((n * PER_CHUNK,)),
        pltpu.SemaphoreType.DMA((2 + n,)),
    ]
    out = pl.pallas_call(
        lambda *refs: kernel(scale, *refs),
        out_shape=jax.ShapeDtypeStruct((16, BLK, k), BF16),
        in_specs=[pl.BlockSpec(memory_space=pl.ANY)] * 2,
        out_specs=pl.BlockSpec(memory_space=pl.ANY),
        scratch_shapes=scratch,
        compiler_params=pltpu.CompilerParams(
            collective_id=0, has_side_effects=True, vmem_limit_bytes=60 * 2**20
        ),
        cost_estimate=pl.CostEstimate(flops=6 * 10**9, bytes_accessed=4 * 2**20, transcendentals=0),
        name="update",
    )(features, panel)
    return out.reshape(width, k).astype(F32)


def solution(mesh):
    return jax.shard_map(
        body,
        mesh=mesh,
        in_specs=(P("sample", "feat"), P("feat", None)),
        out_specs=P("feat", None),
        check_vma=False,
    )
```

time: 79.2 us -> 76.1 us (0.961)
  Pallas kernels: 76.3 us -> 73.1 us
    pallas_call x1, Pallas kernels: 76.3 us -> 73.1 us  [body(): pl.pallas_call(lambda *refs: kernel(scale, *refs), out_shape=jax.ShapeDty...]
where the time goes in v3:
time: 76.1 us; the launch traced here: 75.9 us
  Pallas kernels  73.1 us (96%)
  other arithmetic  2.79 us (4%)
    pallas_call x1, Pallas kernels, body(): pl.pallas_call(lambda *refs: kernel(scale, *refs), out_shape=jax.ShapeDty...  73.1 us
    convert_element_type x1, other arithmetic, body(): return out.reshape(width, k).astype(F32)  2.79 us

profile of v3, /device:TPU:2, one launch (start us, length us, event | category | flops | bytes accessed | tf_op | source)
XLA Modules:
  0.0 75.9 jit_solution(12538937332233269551)
XLA Ops:
  0.0 73.1 %update.1 = bf16[16,32,1024]{2,1,0:T(8,128)(2,1)} custom-call(bf16[1024,512]{1,0:T(8,128)(2,1)} %refs_0_.1, bf16[512,1024]{1,0:T(8,128)(2,1)} %refs_1_.1), custom_call_target="tpu_custom_call" | custom-call | flops 6000000000 | bytes 4194304 | tf_op jit(solution)/shard_map/update/pallas_call | solution.py:272
  73.1 2.8 %bitcast_convert_fusion = f32[512,1024]{1,0:T(8,128)} fusion(bf16[16,32,1024]{2,1,0:T(8,128)(2,1)} %update.1), kind=kLoop, calls=%fused_computation | loop fusion | flops 524288 | bytes 3145728 | tf_op jit(solution)/shard_map/convert_element_type | solution.py:284

commit v4 on v3

v4 whole, which is shorter than its diff:
```python
import math

import jax
import jax.numpy as jnp
from jax import lax
from jax.experimental import pallas as pl
from jax.experimental.pallas import tpu as pltpu
from jax.sharding import PartitionSpec as P

MESH = pl.DeviceIdType.MESH
F32, BF16 = jnp.float32, jnp.bfloat16
D = 8192
WIDTHS = (128, 256, 256, 256, 128)
CHUNKS = len(WIDTHS)
START = tuple(sum(WIDTHS[:c]) for c in range(CHUNKS + 1))
PER_CHUNK = 45
TURN = 4
PIECES = 2
ORDER = (0, 1, 0, 1, 2, 0, 2, 3, 1, 4, 0, 3, 2, 1, 0, 3, 4, 1, 0, 2, 0, 4, 3, 1, 2, 1, 0, 2, 3, 4, 2, 3, 0, 1, 4, 3, 0, 2, 4, 1, 4, 3, 4, 0, 1, 3, 2, 4, 1, 3, 2, 0, 4, 1, 3, 2, 4, 3, 2, 4)
BLK = 32
LAST = -1
NEAR = (1, 7, 2, 6, 3, 5, 4)


def dot(a, b):
    return jnp.dot(a, b, preferred_element_type=F32)


def kernel(scale, f_hbm, v_hbm, out_hbm, fv, ft, vv, part, part_in, psum, l1, t2, l2, proj, projt, wf,
           half_out, half_in, zs_out, zs_in, ob, send_sem, recv_sem, local_sem):
    s, f = lax.axis_index("sample"), lax.axis_index("feat")
    xl, z = s // 8, s % 8
    xh, y, core = f // 8, (f // 2) % 4, f % 2
    q = y // 2
    p = (y + q) % 2
    half = fv.shape[1] // 2

    def feat_dev(xh_, y_, core_):
        return (s, xh_ * 8 + y_ * 2 + core_)

    def sample_dev(xl_, z_):
        return (xl_ * 8 + z_, f)

    y_a = y + 1 - 2 * (y % 2)
    y_b = 3 - y
    sib = feat_dev(xh, y, 1 - core)
    dev_a, dev_b = feat_dev(xh, y_a, core), feat_dev(xh, y_b, core)
    dev_x = feat_dev(1 - xh, y, core)
    dev_l = sample_dev(1 - xl, z)
    dev_ax, dev_bx = feat_dev(1 - xh, y_a, core), feat_dev(1 - xh, y_b, core)
    ring = {k: sample_dev(xl, (z + k) % 8) for k in range(1, 8)}

    loads = [pltpu.make_async_copy(v_hbm, vv, local_sem.at[0]), pltpu.make_async_copy(f_hbm, fv, local_sem.at[1])]
    for load in loads:
        load.start()

    barrier = pltpu.get_barrier_semaphore()
    for partner in (sib, dev_a, dev_b, dev_x, dev_ax, dev_bx, dev_l, *ring.values()):
        pl.semaphore_signal(barrier, inc=1, device_id=partner, device_id_type=MESH)
    for load in loads:
        load.wait()

    def partial(c, side):
        rows = fv[pl.ds(pl.multiple_of(side * BLK * 16, BLK * 16), BLK * 16), :]
        return dot(rows, vv[:, START[c]:START[c + 1]]).reshape(16, BLK, WIDTHS[c])

    pl.semaphore_wait(barrier, 14)

    sent = []

    def send(index, src, dst, device):
        copy = pltpu.make_async_remote_copy(
            src_ref=src, dst_ref=dst, send_sem=send_sem.at[index], recv_sem=recv_sem.at[index],
            device_id=device, device_id_type=MESH,
        )
        copy.start()
        sent.append(copy)
        return copy

    state = {}

    def project(c):
        part[c][...] = partial(c, 1 - core)
        state[c, "half"] = send(c * PER_CHUNK, part[c], part_in[c], sib)
        psum[c][...] = partial(c, core)

    def fold(c):
        i = c * PER_CHUNK + 1
        state[c, "half"].wait_recv()
        at = pl.ds((1 - p) * 4, 4)
        psum[c][at] = psum[c][at] + part_in[c][at]
        state[c, "a1"] = send(i, psum[c].at[at], l1[c].at[0], dev_a)
        at = pl.ds(8 + (1 - q) * 4, 4)
        psum[c][at] = psum[c][at] + part_in[c][at]
        state[c, "b1"] = send(i + 1, psum[c].at[at], l1[c].at[1], dev_b)
        for at in (pl.ds(p * 4, 4), pl.ds(8 + q * 4, 4)):
            psum[c][at] = psum[c][at] + part_in[c][at]
        if c == TURN:
            ft[...] = fv[...].T

    def halve2(c):
        i = c * PER_CHUNK + 3
        state[c, "a1"].wait_recv()
        for slot, at in enumerate((q * 2 + 1 - xh, (1 - q) * 2 + 1 - xh, (1 - q) * 2 + xh, q * 2 + xh)):
            t2[c][2 * slot] = psum[c][p * 4 + at] + l1[c][0, at]
        copies = [
            send(i, t2[c].at[2], l2[c].at[2], dev_bx),
            send(i + 1, t2[c].at[4], l2[c].at[4], dev_b),
        ]
        state[c, "b1"].wait_recv()
        for slot, at in enumerate((p * 2 + 1 - xh, (1 - p) * 2 + 1 - xh, (1 - p) * 2 + xh, p * 2 + xh)):
            t2[c][2 * slot + 1] = psum[c][8 + q * 4 + at] + l1[c][1, at]
        copies += [
            send(i + 2, t2[c].at[3], l2[c].at[3], dev_ax),
            send(i + 3, t2[c].at[pl.ds(0, 2)], l2[c].at[pl.ds(0, 2)], dev_x),
            send(i + 4, t2[c].at[5], l2[c].at[5], dev_a),
        ]
        state[c, "r2"] = copies

    def share(c):
        i = c * PER_CHUNK + 8
        for copy in state[c, "r2"]:
            copy.wait_recv()
        total = (t2[c][6:8] + l2[c][0:2] + l2[c][2:4] + l2[c][4:6]).astype(BF16)
        at_a = p * 4 + q * 2 + xh
        at_b = 8 + q * 4 + p * 2 + xh
        proj[c][core, at_a] = total[0]
        proj[c][core, at_b] = total[1]
        a, b = proj[c].at[core, at_a], proj[c].at[core, at_b]
        state[c, "g2"] = [
            send(i, a, a, dev_bx),
            send(i + 1, b, b, dev_ax),
            send(i + 2, a, a, dev_x),
            send(i + 3, b, b, dev_x),
            send(i + 4, a, a, dev_b),
            send(i + 5, b, b, dev_a),
        ]

    def spread4(c):
        i = c * PER_CHUNK + 14
        for copy in state[c, "g2"]:
            copy.wait_recv()
        a = proj[c].at[core, pl.ds(p * 4, 4)]
        b = proj[c].at[core, pl.ds(8 + q * 4, 4)]
        state[c, "g4"] = [send(i, a, a, dev_a), send(i + 1, b, b, dev_b)]

    def spread_core(c):
        for copy in state[c, "g4"]:
            copy.wait_recv()
        a = proj[c].at[core]
        state[c, "sib"] = send(c * PER_CHUNK + 16, a, a, sib)

    def local_update(c):
        state[c, "sib"].wait_recv()
        pc = proj[c][...].reshape(1024, WIDTHS[c])
        projt[START[c]:START[c + 1], :] = pc.T
        gram = dot(projt[0:START[c + 1], :], pc)
        j = lax.broadcasted_iota(jnp.int32, gram.shape, 0)
        k = lax.broadcasted_iota(jnp.int32, gram.shape, 1) + START[c]
        upper = jnp.where(j <= k, gram, 0.0)
        high = upper.astype(BF16)
        low = (upper - high.astype(F32)).astype(BF16)

        def rows_of(side):
            at = pl.ds(pl.multiple_of(side * half, half), half)
            rows = vv[at, 0:START[c + 1]]
            total = (dot(ft[at, :], pc) - (dot(rows, high) + dot(rows, low))) * scale
            return total.reshape(8, BLK, WIDTHS[c])

        half_out[c][...] = rows_of(1 - xl).astype(BF16)
        state[c, "xl"] = send(c * PER_CHUNK + 20, half_out[c], half_in[c], dev_l)
        wf[c][...] = rows_of(xl)

    def scatter(c):
        i = c * PER_CHUNK + 21
        state[c, "xl"].wait_recv()
        both = wf[c][...] + half_in[c][...].astype(F32)
        wf[c][...] = both
        zs_out[c][...] = both.astype(BF16)
        state[c, "zs"] = [
            send(i + k, zs_out[c].at[(z + k) % 8], zs_in[c].at[k - 1], ring[k]) for k in (4, 3, 5, 2, 6, 1, 7)
        ]

    def finish(c):
        i = c * PER_CHUNK + 29
        for copy in state[c, "zs"]:
            copy.wait_recv()
        total = wf[c][z]
        for k in range(7):
            total = total + zs_in[c][k].astype(F32)
        at = xl * 8 + z
        ob[c][at] = total.astype(BF16)
        a = ob[c].at[at]
        if c == LAST:
            state[c, "ox"] = [send(i + 7, a, a, dev_l)]
            state[c, "o1"] = [send(i + n, a, a, ring[k]) for n, k in enumerate(NEAR)]
            return
        state[c, "o1"] = [send(i + n, a, a, ring[k]) for n, k in enumerate((2, 6, 1, 7))]
        state[c, "ox"] = [send(i + 4, a, a, dev_l)]

    def own(c, k):
        return ob[c].at[xl * 8 + (z + k) % 8]

    def relay(c, first, last):
        i = c * PER_CHUNK + 37
        for n in range(first, last):
            state[c, "o1"][n].wait_recv()
            a = own(c, (8 - NEAR[n]) % 8)
            state[c, "ox"] += [send(i + n, a, a, dev_l)]

    def gather2(c):
        if c == LAST:
            return relay(c, 0, 4)
        i = c * PER_CHUNK + 34
        up2, down2, up1, down1 = state[c, "o1"]
        down1.wait_recv()
        up2.wait_recv()
        a, b = own(c, 1), own(c, 6)
        state[c, "o2"] = [send(i, a, a, ring[6])]
        b2 = b.at[pl.ds(0, BLK // 2)]
        state[c, "o2"] += [send(i + 1, b2, b2, ring[2])]
        up1.wait_recv()
        down2.wait_recv()
        a, b = own(c, 7), own(c, 2)
        state[c, "o2"] += [send(i + 2, a, a, ring[2])]
        b2 = b.at[pl.ds(BLK // 2, BLK // 2)]
        state[c, "o2"] += [send(i + 3, b2, b2, ring[6])]
        for n, k in enumerate((1, 7, 2, 6)):
            a = own(c, k)
            state[c, "ox"] += [send(i + 4 + n, a, a, dev_l)]

    def swap(c):
        if c == LAST:
            return relay(c, 4, 7)
        i = c * PER_CHUNK + 42
        for copy in state[c, "o2"]:
            copy.wait_recv()
        for n, k in enumerate((3, 4, 5)):
            a = own(c, k)
            state[c, "ox"] += [send(i + n, a, a, dev_l)]

    def write(c):
        for copy in state[c, "ox"]:
            copy.wait_recv()
        copy = pltpu.make_async_copy(ob[c], out_hbm.at[:, :, START[c]:START[c + 1]], local_sem.at[2 + c])
        copy.start()
        state[c, "out"] = copy

    stages = [project, fold, halve2, share, spread4, spread_core, local_update, scatter, finish, gather2, swap, write]
    done = [0] * CHUNKS
    for c in ORDER:
        stages[done[c]](c)
        done[c] += 1
    for copy in sent:
        copy.wait_send()
    for c in range(CHUNKS):
        state[c, "out"].wait()


def widen_kernel(x_ref, o_ref):
    o_ref[...] = x_ref[...].astype(F32)


def widen(x):
    rows, k = x.shape
    tile = rows // PIECES
    spec = pl.BlockSpec((tile, k), lambda i: (i, 0))
    return pl.pallas_call(
        widen_kernel,
        grid=(PIECES,),
        out_shape=jax.ShapeDtypeStruct((rows, k), F32),
        in_specs=[spec],
        out_specs=spec,
        name="widen",
    )(x)


def body(features, panel):
    rows, width = features.shape
    k = panel.shape[1]
    n = CHUNKS
    scale = math.sqrt(D) / (rows * lax.axis_size("sample"))
    scratch = [
        pltpu.VMEM((rows, width), BF16),
        pltpu.VMEM((width, rows), BF16),
        pltpu.VMEM((width, k), BF16),
        [pltpu.VMEM((16, BLK, w), F32) for w in WIDTHS],
        [pltpu.VMEM((16, BLK, w), F32) for w in WIDTHS],
        [pltpu.VMEM((16, BLK, w), F32) for w in WIDTHS],
        [pltpu.VMEM((2, 4, BLK, w), F32) for w in WIDTHS],
        [pltpu.VMEM((8, BLK, w), F32) for w in WIDTHS],
        [pltpu.VMEM((6, BLK, w), F32) for w in WIDTHS],
        [pltpu.VMEM((2, 16, BLK, w), BF16) for w in WIDTHS],
        pltpu.VMEM((k, rows), BF16),
        [pltpu.VMEM((8, BLK, w), F32) for w in WIDTHS],
        [pltpu.VMEM((8, BLK, w), BF16) for w in WIDTHS],
        [pltpu.VMEM((8, BLK, w), BF16) for w in WIDTHS],
        [pltpu.VMEM((8, BLK, w), BF16) for w in WIDTHS],
        [pltpu.VMEM((7, BLK, w), BF16) for w in WIDTHS],
        [pltpu.VMEM((16, BLK, w), BF16) for w in WIDTHS],
        pltpu.SemaphoreType.DMA((n * PER_CHUNK,)),
        pltpu.SemaphoreType.DMA((n * PER_CHUNK,)),
        pltpu.SemaphoreType.DMA((2 + n,)),
    ]
    out = pl.pallas_call(
        lambda *refs: kernel(scale, *refs),
        out_shape=jax.ShapeDtypeStruct((16, BLK, k), BF16),
        in_specs=[pl.BlockSpec(memory_space=pl.ANY)] * 2,
        out_specs=pl.BlockSpec(memory_space=pl.ANY),
        scratch_shapes=scratch,
        compiler_params=pltpu.CompilerParams(
            collective_id=0, has_side_effects=True, vmem_limit_bytes=60 * 2**20
        ),
        cost_estimate=pl.CostEstimate(flops=6 * 10**9, bytes_accessed=4 * 2**20, transcendentals=0),
        name="update",
    )(features, panel)
    return widen(out.reshape(width, k))


def solution(mesh):
    return jax.shard_map(
        body,
        mesh=mesh,
        in_specs=(P("sample", "feat"), P("feat", None)),
        out_specs=P("feat", None),
        check_vma=False,
    )
```

time: 76.1 us -> 75.2 us (0.988)
  other arithmetic: 2.79 us -> 0 us
  Pallas kernels: 73.1 us -> 75.1 us
    convert_element_type x1 -> x0, other arithmetic: 2.79 us -> none  [body(): return out.reshape(width, k).astype(F32)]
    pallas_call x0 -> x1, Pallas kernels: none -> 2.44 us  [widen(): pl.pallas_call(widen_kernel, grid=(PIECES,), out_shape=jax.ShapeDtypeStru...]
where the time goes in v4:
time: 75.2 us; the launch traced here: 75.1 us
  Pallas kernels  75.1 us (100%)
    pallas_call x1, Pallas kernels, body(): pl.pallas_call(lambda *refs: kernel(scale, *refs), out_shape=jax.ShapeDty...  72.6 us
    pallas_call x1, Pallas kernels, widen(): pl.pallas_call(widen_kernel, grid=(PIECES,), out_shape=jax.ShapeDtypeStru...  2.44 us

profile of v4, /device:TPU:2, one launch (start us, length us, event | category | flops | bytes accessed | tf_op | source)
XLA Modules:
  0.0 75.1 jit_solution(14434592674389034385)
XLA Ops:
  0.0 72.6 %update.1 = bf16[16,32,1024]{2,1,0:T(8,128)(2,1)} custom-call(bf16[1024,512]{1,0:T(8,128)(2,1)} %refs_0_.1, bf16[512,1024]{1,0:T(8,128)(2,1)} %refs_1_.1), custom_call_target="tpu_custom_call" | custom-call | flops 6000000000 | bytes 4194304 | tf_op jit(solution)/shard_map/update/pallas_call | solution.py:305
  72.6 2.4 %widen.1 = f32[512,1024]{1,0:T(8,128)} custom-call(bf16[512,1024]{1,0:T(8,128)(2,1)} %bitcast.1), custom_call_target="tpu_custom_call" | custom-call | tf_op jit(solution)/shard_map/widen/pallas_call | solution.py:268
